TPU v7x, 128 devices: a whole 4x4x4 slice. The times are simulated.
128 devices in a mesh: pipe: 16 (over x_lo, z, core), tensor: 8 (over x_hi, y).
Axes of the slice: x: 4 (x_hi: 2, x_lo: 2; x = x_hi * 2 + x_lo), y: 4, z: 4, core: 2. Of those that a mesh axis runs over, the one named last changes fastest.
Arguments:
- stashed: bfloat16 [16, 2, 512, 4096], P('pipe', None, 'tensor'), may hold values from -64 to 64
- upstream: bfloat16 [16, 512, 4096], P('pipe', 'tensor'), may hold values from -6 to 6
- loss_grad: bfloat16 [512, 4096], P('tensor'), may hold values from -6 to 6
- norm_gain: float32 [16, 4096], P('pipe'), may hold values from 0.5 to 1.5
- w_query: bfloat16 [16, 4096, 4096], P('pipe', None, 'tensor'), may hold values from -0.09375 to 0.09375
- w_key: bfloat16 [16, 4096, 1024], P('pipe', None, 'tensor'), may hold values from -2.359375 to 2.359375
- w_value: bfloat16 [16, 4096, 1024], P('pipe', None, 'tensor'), may hold values from -0.09375 to 0.09375
- w_out: bfloat16 [16, 4096, 4096], P('pipe', 'tensor'), may hold values from -0.09375 to 0.09375
- evicted_map: int32 [16], replicated, may hold values from 0 to 1, as said below
- plan: int32 [17], replicated, may hold values from 0 to 16, each once
- segments: int32 [17, 512], replicated, may hold values from 0 to 3, never falling along the last dimension, each value on 1 to 256 neighbouring positions
Outputs:
- layer_grads: bfloat16 [16, 2, 512, 4096], P('pipe', None, 'tensor')
Inputs may be any that keep to these rules, and one draw needn't show every extreme that they name: `evicted_map`: entry i equals entry 15 - i and entry 0 is 1; where entry i is 1, stashed[i] holds the inputs of section 15 - i.
All inputs are finite; a program needn't handle non-finite values.
Results may differ from a plain program's by a relative error of at most 0.023.
The roundings to bfloat16 on the way count: a program that leaves them out, or rounds other values in their place, can miss the bound.
Values may be sent and summed in bfloat16 or wider, within the bound.
A program may use at most 128 MiB of HBM per device.

v0:
```python
import math

import jax
import jax.numpy as jnp
from jax import lax
from jax.experimental import pallas as pl
from jax.experimental.pallas import tpu as pltpu
from jax.sharding import PartitionSpec as P

MESH = pl.DeviceIdType.MESH
HD = 128
EPS = 1e-05
F32 = jnp.float32
BF16 = jnp.bfloat16


class Net:
    def __init__(self, send, recv):
        self.send, self.recv, self.used = send, recv, 0

    def copy(self, src, dst, device):
        i = self.used
        self.used += 1
        return pltpu.make_async_remote_copy(
            src_ref=src,
            dst_ref=dst,
            send_sem=self.send.at[i],
            recv_sem=self.recv.at[i],
            device_id=device,
            device_id_type=MESH,
        )


def kernel(
    stash, upstream, loss, gain, wq, wk, wv, wo, evicted, plan, segs, out,
    w, wout, h0, d0, h1, d1, part, r0, r1, own, mir, lossv, pas, res,
    qs, ogs, kk, vv, dqkv, dk_acc, dv_acc, lsem, ssem, rsem,
):
    p, t = lax.axis_index("pipe"), lax.axis_index("tensor")
    xh, y = t // 4, t % 4
    yp, ym, y2 = (y + 1) % 4, (y + 3) % 4, (y + 2) % 4
    xo = 1 - xh
    to_yp, to_ym, to_x = (p, xh * 4 + yp), (p, xh * 4 + ym), (p, xo * 4 + y)
    to_mirror, to_prev, from_next = (15 - p, t), ((p + 15) % 16, t), ((p + 1) % 16, t)
    net = Net(ssem, rsem)

    def rows(a, b, h):
        return pl.ds(pl.multiple_of((a * 4 + b) * 64 + 32 * h, 32), 32)

    mine = pl.ds(pl.multiple_of(t * 64, 64), 64)

    barrier = pltpu.get_barrier_semaphore()
    for device in (to_yp, to_ym, to_x, to_mirror, from_next):
        pl.semaphore_signal(barrier, inc=1, device_id=device, device_id_type=MESH)

    local = [
        pltpu.make_async_copy(upstream.at[0], d0.at[mine], lsem.at[0]),
        pltpu.make_async_copy(stash.at[0], own, lsem.at[1]),
        pltpu.make_async_copy(wo.at[0], wout, lsem.at[2]),
        pltpu.make_async_copy(wq.at[0], w.at[:, 0:512], lsem.at[3]),
        pltpu.make_async_copy(wk.at[0], w.at[:, 512:640], lsem.at[4]),
        pltpu.make_async_copy(wv.at[0], w.at[:, 640:768], lsem.at[5]),
        pltpu.make_async_copy(loss, lossv, lsem.at[6]),
    ]
    for c in local:
        c.start()
    pl.semaphore_wait(barrier, 5)

    class Gather:
        def __init__(self, g):
            def cp(sl, device):
                return net.copy(g.at[sl], g.at[sl], device)

            self.x = [cp(rows(xh, y, h), to_x) for h in (0, 1)]
            self.a_p = [cp(rows(xh, y, h), to_yp) for h in (0, 1)]
            self.a_m = [cp(rows(xh, y, h), to_ym) for h in (0, 1)]
            self.b_p = [cp(rows(xo, y, h), to_yp) for h in (0, 1)]
            self.b_m = [cp(rows(xo, y, h), to_ym) for h in (0, 1)]
            self.c_p = cp(rows(xh, ym, 0), to_yp)
            self.c_m = cp(rows(xo, yp, 1), to_ym)
            self.e_0 = cp(rows(xh, y2, 0), to_x)
            self.e_1 = cp(rows(xo, y2, 1), to_x)

        def first(self, h):
            self.x[h].start()
            self.a_p[h].start()
            self.a_m[h].start()

        def ev(self, i):
            if i == 0:
                self.first(0)
                self.first(1)
            elif i == 1 or i == 3:
                h = i // 2
                self.x[h].wait_recv()
                self.b_p[h].start()
                self.b_m[h].start()
            elif i == 2:
                self.a_p[0].wait_recv()
                self.c_p.start()
            elif i == 4:
                self.b_m[1].wait_recv()
                self.c_m.start()
            elif i == 5:
                self.c_p.wait_recv()
                self.e_0.start()
            elif i == 6:
                self.c_m.wait_recv()
                self.e_1.start()
            else:
                for c in [self.a_p[1], *self.a_m, *self.b_p, self.b_m[0], self.e_0, self.e_1]:
                    c.wait_recv()

        def drain(self):
            for c in [*self.x, *self.a_p, *self.a_m, *self.b_p, *self.b_m, self.c_p, self.c_m, self.e_0, self.e_1]:
                c.wait_send()

    class Scatter:
        def __init__(self, r):
            def cp(sl, slot, device):
                return net.copy(part.at[sl], r.at[pl.ds(32 * slot, 32)], device)

            self.r = r
            self.c = [
                cp(rows(xo, y2, 0), 0, to_x),
                cp(rows(xh, y2, 1), 1, to_x),
                cp(rows(xh, y2, 0), 2, to_ym),
                cp(rows(xo, y2, 1), 3, to_yp),
                cp(rows(xo, ym, 0), 4, to_ym),
                cp(rows(xo, ym, 1), 5, to_ym),
                cp(rows(xo, yp, 0), 6, to_yp),
                cp(rows(xo, yp, 1), 7, to_yp),
                cp(rows(xh, ym, 0), 8, to_ym),
                cp(rows(xh, ym, 1), 9, to_ym),
                cp(rows(xh, yp, 0), 10, to_yp),
                cp(rows(xh, yp, 1), 11, to_yp),
                cp(rows(xo, y, 0), 12, to_x),
                cp(rows(xo, y, 1), 13, to_x),
            ]

        def start(self, *ids):
            for i in ids:
                self.c[i].start()

        def add(self, sl, *slots):
            for i in slots:
                self.c[i].wait_recv()

            def body(n, carry):
                cols = pl.ds(pl.multiple_of(n * 512, 512), 512)
                total = part[sl, cols].astype(F32)
                for i in slots:
                    total = total + self.r[pl.ds(32 * i, 32), cols].astype(F32)
                part[sl, cols] = total.astype(BF16)
                return carry

            lax.fori_loop(0, 8, body, 0)

        def ev(self, i):
            if i == 1:
                self.add(rows(xh, y2, 0), 0)
                self.start(2)
            elif i == 2:
                self.add(rows(xo, y2, 1), 1)
                self.start(3)
            elif i == 3:
                self.add(rows(xo, y, 0), 4, 6)
                self.start(12)
            elif i == 4:
                self.add(rows(xo, yp, 1), 3)
                self.start(7)
            elif i == 5:
                self.add(rows(xh, ym, 0), 2)
                self.start(8)
            elif i == 6:
                self.add(rows(xo, y, 1), 5, 7)
                self.start(13)

        def drain(self):
            for c in self.c:
                c.wait_send()

    gathers = [Gather(g) for g in (d0, h0, h1, d1)]
    gd0, gh0, gh1, gd1 = gathers
    scatters = [Scatter(r) for r in (r0, r1)]
    mirrors = [
        [net.copy(stash.at[0, m, pl.ds(32 * h, 32)], mir.at[m, pl.ds(32 * h, 32)], to_mirror) for h in (0, 1)]
        for m in (0, 1)
    ]
    passes = [net.copy(res.at[0, pl.ds(32 * h, 32)], pas.at[pl.ds(32 * h, 32)], to_prev) for h in (0, 1)]
    flipped = evicted[p] == 1
    gain_row = gain[...]

    def norm(m, g):
        def body(n, carry):
            sl = pl.ds(pl.multiple_of(n * 16, 16), 16)
            x = jnp.where(flipped, mir[m, sl].astype(F32), own[m, sl].astype(F32))
            own[m, sl] = x.astype(BF16)
            inverse = 1.0 / jnp.sqrt(jnp.mean(x * x, axis=-1, keepdims=True) + EPS)
            g[pl.ds(pl.multiple_of(t * 64 + n * 16, 16), 16)] = (x * inverse * gain_row).astype(BF16)
            return carry

        lax.fori_loop(0, 4, body, 0)

    def norm_back(m, h, g, r):
        def body(n, carry):
            lo = n * 16
            sl = pl.ds(pl.multiple_of(h * 32 + lo, 16), 16)
            row = pl.ds(pl.multiple_of(t * 64 + h * 32 + lo, 16), 16)
            total = part[row].astype(F32)
            for i in (8, 10, 12):
                total = total + r[pl.ds(pl.multiple_of(32 * (i + h) + lo, 16), 16)].astype(F32)
            x = own[m, sl].astype(F32)
            inverse = 1.0 / jnp.sqrt(jnp.mean(x * x, axis=-1, keepdims=True) + EPS)
            normed = x * inverse
            scaled = total * gain_row
            result = inverse * (scaled - normed * jnp.mean(scaled * normed, axis=-1, keepdims=True))
            res[m, sl] = (result + g[row].astype(F32)).astype(BF16)
            return carry

        lax.fori_loop(0, 2, body, 0)

    def project(g):
        def body(n, carry):
            r = jnp.dot(g[pl.ds(pl.multiple_of(n * 256, 256), 256)], w[...], preferred_element_type=F32).astype(BF16)
            sl = pl.ds(pl.multiple_of(n * 256, 256), 256)
            for j in range(4):
                qs[pl.ds(pl.multiple_of(j * 512 + n * 256, 256), 256)] = r[:, j * HD : (j + 1) * HD]
            kk[sl] = r[:, 512:640]
            vv[sl] = r[:, 640:768]
            return carry

        lax.fori_loop(0, 2, body, 0)

    def back_out(g):
        def body(n, carry):
            r = lax.dot_general(
                g[pl.ds(pl.multiple_of(n * 256, 256), 256)], wout[...], (((1,), (1,)), ((), ())),
                preferred_element_type=F32,
            ).astype(BF16)
            for j in range(4):
                ogs[pl.ds(pl.multiple_of(j * 512 + n * 256, 256), 256)] = r[:, j * HD : (j + 1) * HD]
            return carry

        lax.fori_loop(0, 2, body, 0)

    def attend(m):
        seg_row = segs[pl.ds(plan[p + m], 1)]
        seg_col = jnp.broadcast_to(seg_row, (128, 512)).T[:, :1]
        scale = 1.0 / math.sqrt(HD)
        dk_acc[...] = jnp.zeros_like(dk_acc)
        dv_acc[...] = jnp.zeros_like(dv_acc)
        nt = (((1,), (1,)), ((), ()))

        def head(j, carry):
            for b in (0, 1):
                keys = 256 * (b + 1)
                sl = pl.ds(pl.multiple_of(j * 512 + b * 256, 256), 256)
                q, og = qs[sl], ogs[sl]
                k, v = kk[:keys], vv[:keys]
                scores = lax.dot_general(k, q, nt, preferred_element_type=F32) * scale
                kpos = lax.broadcasted_iota(jnp.int32, (keys, 256), 0)
                qpos = lax.broadcasted_iota(jnp.int32, (keys, 256), 1) + b * 256
                allowed = (kpos <= qpos) & (seg_col[:keys] == seg_row[:, b * 256 : (b + 1) * 256])
                scores = jnp.where(allowed, scores, -1e30)
                weights = jnp.exp(scores - jnp.max(scores, axis=0, keepdims=True))
                weights = weights * (1.0 / jnp.sum(weights, axis=0, keepdims=True))
                weight_grad = lax.dot_general(v, og, nt, preferred_element_type=F32)
                delta = jnp.sum(weights * weight_grad, axis=0, keepdims=True)
                score_grad = (weights * (weight_grad - delta) * scale).astype(BF16)
                dv_acc[:keys] += jnp.dot(weights.astype(BF16), og, preferred_element_type=F32)
                dk_acc[:keys] += jnp.dot(score_grad, q, preferred_element_type=F32)
                dq = jnp.dot(k.T, score_grad, preferred_element_type=F32)
                dqkv[j, b * 256 : (b + 1) * 256] = dq.T.astype(BF16)
            return carry

        lax.fori_loop(0, 4, head, 0)
        dqkv[4] = dk_acc[...].astype(BF16)
        dqkv[5] = dv_acc[...].astype(BF16)

    def back_in(b):
        lo, hi = [pl.ds(pl.multiple_of(a * 256 + b * 64, 64), 64) for a in (0, 1)]
        lhs = jnp.concatenate(
            [jnp.concatenate([dqkv[j, sl] for j in range(6)], axis=1) for sl in (lo, hi)], axis=0
        )

        def body(n, carry):
            cols = pl.ds(pl.multiple_of(n * 512, 512), 512)
            r = lax.dot_general(
                lhs, w[cols], (((1,), (1,)), ((), ())), preferred_element_type=F32
            ).astype(BF16)
            part[lo, cols] = r[:64]
            part[hi, cols] = r[64:]
            return carry

        lax.fori_loop(0, 8, body, 0)

    def scatter_first(sc):
        back_in(y2)
        sc.start(0, 1)
        back_in(ym)
        sc.start(4, 5, 9)
        back_in(yp)
        sc.start(6, 10, 11)
        back_in(y)

    for c in mirrors[0]:
        c.start()
    local[0].wait()
    gd0.ev(0)
    gd0.ev(1)
    gd0.ev(2)
    local[1].wait()
    for c in mirrors[0]:
        c.wait_recv()
    norm(0, h0)
    gh0.ev(0)
    for c in mirrors[1]:
        c.start()
    gd0.ev(3)
    gd0.ev(4)
    gh0.ev(1)
    gh0.ev(2)
    gd0.ev(5)
    gd0.ev(6)
    gh0.ev(3)
    gd0.ev(7)
    for c in local[2:]:
        c.wait()
    gh0.ev(4)
    back_out(d0)
    gh0.ev(5)
    for c in mirrors[1]:
        c.wait_recv()
    norm(1, h1)
    gh0.ev(6)
    gh1.ev(0)
    gh0.ev(7)
    project(h0)
    gh1.ev(1)
    gh1.ev(2)
    attend(0)
    gh1.ev(3)
    gh1.ev(4)
    sc = scatters[0]
    scatter_first(sc)
    gh1.ev(5)
    gh1.ev(6)
    sc.ev(1)
    sc.ev(2)
    sc.ev(3)
    sc.ev(4)
    sc.ev(5)
    sc.ev(6)
    gh1.ev(7)
    project(h1)
    for h in (0, 1):
        for i in (8, 10, 12):
            sc.c[i + h].wait_recv()
        norm_back(0, h, d0, r0)
        passes[h].start()
    first_out = pltpu.make_async_copy(res.at[0], out.at[0, 0], lsem.at[7])
    first_out.start()

    last = p == 15
    for h in (0, 1):
        passes[h].wait_recv()
        sl = pl.ds(32 * h, 32)
        d1[rows(xh, y, h)] = jnp.where(last, lossv[sl].astype(F32), pas[sl].astype(F32)).astype(BF16)
        gd1.first(h)
    for i in range(1, 8):
        gd1.ev(i)
    sc.drain()
    back_out(d1)
    attend(1)
    sc = scatters[1]
    scatter_first(sc)
    for i in range(1, 7):
        sc.ev(i)
    for h in (0, 1):
        for i in (8, 10, 12):
            sc.c[i + h].wait_recv()
        norm_back(1, h, d1, r1)
    second_out = pltpu.make_async_copy(res.at[1], out.at[0, 1], lsem.at[8])
    second_out.start()
    sc.drain()
    for g in gathers:
        g.drain()
    for c in [*mirrors[0], *mirrors[1], *passes]:
        c.wait_send()
    first_out.wait()
    second_out.wait()


def on_device(stashed, upstream, loss_grad, norm_gain, w_query, w_key, w_value, w_out, evicted_map, plan, segments):
    hbm = pl.BlockSpec(memory_space=pl.ANY)
    vmem = pl.BlockSpec(memory_space=pltpu.VMEM)
    smem = pl.BlockSpec(memory_space=pltpu.SMEM)
    full = pltpu.VMEM((512, 4096), BF16)
    return pl.pallas_call(
        kernel,
        name="relay_backward",
        out_shape=jax.ShapeDtypeStruct((1, 2, 64, 4096), BF16),
        in_specs=[hbm, hbm, hbm, vmem, hbm, hbm, hbm, hbm, smem, smem, vmem],
        out_specs=hbm,
        scratch_shapes=[
            pltpu.VMEM((4096, 768), BF16),
            full, full, full, full, full, full,
            pltpu.VMEM((448, 4096), BF16),
            pltpu.VMEM((448, 4096), BF16),
            pltpu.VMEM((2, 64, 4096), BF16),
            pltpu.VMEM((2, 64, 4096), BF16),
            pltpu.VMEM((64, 4096), BF16),
            pltpu.VMEM((64, 4096), BF16),
            pltpu.VMEM((2, 64, 4096), BF16),
            pltpu.VMEM((2048, HD), BF16),
            pltpu.VMEM((2048, HD), BF16),
            pltpu.VMEM((512, HD), BF16),
            pltpu.VMEM((512, HD), BF16),
            pltpu.VMEM((6, 512, HD), BF16),
            pltpu.VMEM((512, HD), F32),
            pltpu.VMEM((512, HD), F32),
            pltpu.SemaphoreType.DMA((9,)),
            pltpu.SemaphoreType.DMA((90,)),
            pltpu.SemaphoreType.DMA((90,)),
        ],
        compiler_params=pltpu.CompilerParams(
            collective_id=0, has_side_effects=True, vmem_limit_bytes=60 * 2**20
        ),
        cost_estimate=pl.CostEstimate(flops=20 * 10**9, bytes_accessed=16 * 2**20, transcendentals=2 * 10**6),
    )(stashed, upstream, loss_grad, norm_gain, w_query, w_key, w_value, w_out, evicted_map, plan, segments)


def solution(mesh):
    in_specs = (
        P("pipe", None, "tensor", None),
        P("pipe", "tensor", None),
        P("tensor", None),
        P("pipe", None),
        P("pipe", None, "tensor"),
        P("pipe", None, "tensor"),
        P("pipe", None, "tensor"),
        P("pipe", "tensor", None),
        P(),
        P(),
        P(),
    )
    return jax.shard_map(
        on_device, mesh=mesh, in_specs=in_specs, out_specs=P("pipe", None, "tensor", None), check_vma=False
    )
```

profile of v0, /device:TPU:0, one launch (start us, length us, event | category | flops | bytes accessed | tf_op | source)
XLA Modules:
  0.0 248.8 jit_solution(2746850660449701690)
XLA Ops:
  0.0 246.5 %relay_backward.1 = bf16[1,2,64,4096]{3,2,1,0:T(8,128)(2,1)} custom-call(bf16[1,2,64,4096]{3,2,1,0:T(8,128)(2,1)} %stash.1, bf16[1,64,4096]{2,1,0:T(8,128)(2,1)} %upstream.1, bf16[64,4096]{1,0:T(8,128)(2,1)} %loss.1, f32[1,4096]{1,0:T(1,128)} %gain.1, bf16[1,4096,512]{2,1,0:T(8,128)(2,1)} %wq.1, bf16[1,4096,128]{2,1,0:T(8,128)(2,1)} %wk.1, ...), custom_call_target="tpu_custom_call" | custom-call | flops 20000000000 | bytes 16777216 | tf_op jit(solution)/shard_map/relay_backward/pallas_call | solution.py:400
  246.5 2.3 copy.13
where the time goes:
time: 249 us
  Pallas kernels  247 us (99%)
    pallas_call x1, Pallas kernels, on_device(): pl.pallas_call(kernel, name='relay_backward', out_shape=jax.ShapeDtypeStr...  247 us

commit v1 on v0

v1 whole, which is shorter than its diff:
```python
import math

import jax
import jax.numpy as jnp
from jax import lax
from jax.experimental import pallas as pl
from jax.experimental.pallas import tpu as pltpu
from jax.sharding import PartitionSpec as P

MESH = pl.DeviceIdType.MESH
HD = 128
EPS = 1e-05
F32 = jnp.float32
BF16 = jnp.bfloat16


class Net:
    def __init__(self, send, recv):
        self.send, self.recv, self.used = send, recv, 0

    def copy(self, src, dst, device):
        i = self.used
        self.used += 1
        return pltpu.make_async_remote_copy(
            src_ref=src,
            dst_ref=dst,
            send_sem=self.send.at[i],
            recv_sem=self.recv.at[i],
            device_id=device,
            device_id_type=MESH,
        )


def kernel(
    stash, upstream, loss, gain, wq, wk, wv, wo, evicted, plan, segs, out,
    w, wout, h0, d0, h1, d1, part, r0, r1, own, mir, lossv, pas, res,
    qs, ogs, kk, vv, dqkv, dk_acc, dv_acc, bias, probs, lsem, ssem, rsem,
):
    p, t = lax.axis_index("pipe"), lax.axis_index("tensor")
    xh, y = t // 4, t % 4
    yp, ym, y2 = (y + 1) % 4, (y + 3) % 4, (y + 2) % 4
    xo = 1 - xh
    to_yp, to_ym, to_x = (p, xh * 4 + yp), (p, xh * 4 + ym), (p, xo * 4 + y)
    to_mirror, to_prev, from_next = (15 - p, t), ((p + 15) % 16, t), ((p + 1) % 16, t)
    net = Net(ssem, rsem)

    def rows(a, b, h):
        return pl.ds(pl.multiple_of((a * 4 + b) * 64 + 32 * h, 32), 32)

    def part_rows(a, b, h, q):
        return pl.ds(pl.multiple_of((a * 4 + b) * 64 + 32 * h + 16 * q, 16), 16)

    mine = pl.ds(pl.multiple_of(t * 64, 64), 64)

    barrier = pltpu.get_barrier_semaphore()
    for device in (to_yp, to_ym, to_x, to_mirror, from_next):
        pl.semaphore_signal(barrier, inc=1, device_id=device, device_id_type=MESH)

    local = [
        pltpu.make_async_copy(upstream.at[0], d0.at[mine], lsem.at[0]),
        pltpu.make_async_copy(stash.at[0], own, lsem.at[1]),
        pltpu.make_async_copy(wo.at[0], wout, lsem.at[2]),
        pltpu.make_async_copy(wq.at[0], w.at[:, 0:512], lsem.at[3]),
        pltpu.make_async_copy(wk.at[0], w.at[:, 512:640], lsem.at[4]),
        pltpu.make_async_copy(wv.at[0], w.at[:, 640:768], lsem.at[5]),
        pltpu.make_async_copy(loss, lossv, lsem.at[6]),
    ]
    for c in local:
        c.start()
    pl.semaphore_wait(barrier, 5)

    class Gather:
        def __init__(self, g, h, along=False):
            def cp(sl, device):
                return net.copy(g.at[sl], g.at[sl], device)

            self.along = along
            self.x = cp(rows(xh, y, h), to_x)
            self.a_p, self.a_m = cp(rows(xh, y, h), to_yp), cp(rows(xh, y, h), to_ym)
            self.b_p, self.b_m = cp(rows(xo, y, h), to_yp), cp(rows(xo, y, h), to_ym)
            self.c_p, self.c_m = cp(part_rows(xh, ym, h, 0), to_yp), cp(part_rows(xh, yp, h, 1), to_ym)
            if along:
                self.e_p, self.e_m = cp(part_rows(xo, ym, h, 0), to_yp), cp(part_rows(xo, yp, h, 1), to_ym)
                self.ends = (self.e_p, self.e_m)
            else:
                self.e = cp(rows(xh, y2, h), to_x)
                self.ends = (self.e,)

        def near(self):
            self.a_p.start()
            self.a_m.start()

        def far(self):
            self.a_p.wait_recv()
            self.a_m.wait_recv()
            self.c_p.start()
            self.c_m.start()

        def across(self):
            self.x.wait_recv()
            self.b_p.start()
            self.b_m.start()

        def last(self):
            if self.along:
                self.b_p.wait_recv()
                self.e_p.start()
                self.b_m.wait_recv()
                self.e_m.start()
            else:
                self.c_p.wait_recv()
                self.c_m.wait_recv()
                self.e.start()

        def done(self):
            for c in ((self.c_p, self.c_m) if self.along else (self.b_p, self.b_m)) + self.ends:
                c.wait_recv()

        def drain(self):
            for c in (self.x, self.a_p, self.a_m, self.b_p, self.b_m, self.c_p, self.c_m, *self.ends):
                c.wait_send()

    class Scatter:
        def __init__(self, r, h):
            def cp(sl, lo, n, device):
                return net.copy(part.at[sl], r.at[pl.ds(224 * h + lo, n)], device)

            self.r, self.h = r, h
            self.e = cp(rows(xo, y2, h), 0, 32, to_x)
            self.b_m, self.b_p = cp(rows(xo, ym, h), 32, 32, to_ym), cp(rows(xo, yp, h), 64, 32, to_yp)
            self.c_m = cp(part_rows(xh, y2, h, 0), 96, 16, to_ym)
            self.c_p = cp(part_rows(xh, y2, h, 1), 112, 16, to_yp)
            self.a_m, self.a_p = cp(rows(xh, ym, h), 128, 32, to_ym), cp(rows(xh, yp, h), 160, 32, to_yp)
            self.x = cp(rows(xo, y, h), 192, 32, to_x)

        def add(self, sl, n, *los):
            def body(i, carry):
                cols = pl.ds(pl.multiple_of(i * 512, 512), 512)
                total = part[sl, cols].astype(F32)
                for lo in los:
                    total = total + self.r[pl.ds(224 * self.h + lo, n), cols].astype(F32)
                part[sl, cols] = total.astype(BF16)
                return carry

            lax.fori_loop(0, 8, body, 0)

        def far(self):
            self.e.wait_recv()
            self.add(rows(xh, y2, self.h), 32, 0)
            self.c_m.start()
            self.c_p.start()

        def across(self):
            self.b_m.wait_recv()
            self.b_p.wait_recv()
            self.add(rows(xo, y, self.h), 32, 32, 64)
            self.x.start()

        def near(self):
            self.c_m.wait_recv()
            self.add(part_rows(xh, ym, self.h, 0), 16, 96)
            self.a_m.start()
            self.c_p.wait_recv()
            self.add(part_rows(xh, yp, self.h, 1), 16, 112)
            self.a_p.start()

        def done(self):
            for c in (self.a_m, self.a_p, self.x):
                c.wait_recv()

        def drain(self):
            for c in (self.e, self.b_m, self.b_p, self.c_m, self.c_p, self.a_m, self.a_p, self.x):
                c.wait_send()

    gd0 = [Gather(d0, 0), Gather(d0, 1, along=True)]
    gh0, gh1, gd1 = [[Gather(g, h) for h in (0, 1)] for g in (h0, h1, d1)]
    sc0, sc1 = [[Scatter(r, h) for h in (0, 1)] for r in (r0, r1)]
    mirrors = [
        [net.copy(stash.at[0, m, pl.ds(32 * h, 32)], mir.at[m, pl.ds(32 * h, 32)], to_mirror) for h in (0, 1)]
        for m in (0, 1)
    ]
    passes = [net.copy(res.at[0, pl.ds(32 * h, 32)], pas.at[pl.ds(32 * h, 32)], to_prev) for h in (0, 1)]
    flipped = evicted[p] == 1
    gain_row = gain[...]
    nt = (((1,), (1,)), ((), ()))
    scale = 1.0 / math.sqrt(HD)

    def norm(m, h, g):
        def body(n, carry):
            lo = 32 * h + n * 16
            sl = pl.ds(pl.multiple_of(lo, 16), 16)
            x = jnp.where(flipped, mir[m, sl].astype(F32), own[m, sl].astype(F32))
            own[m, sl] = x.astype(BF16)
            inverse = 1.0 / jnp.sqrt(jnp.mean(x * x, axis=-1, keepdims=True) + EPS)
            g[pl.ds(pl.multiple_of(t * 64 + lo, 16), 16)] = (x * inverse * gain_row).astype(BF16)
            return carry

        lax.fori_loop(0, 2, body, 0)

    def norm_back(m, h, g, r):
        def body(n, carry):
            lo = n * 16
            sl = pl.ds(pl.multiple_of(h * 32 + lo, 16), 16)
            row = pl.ds(pl.multiple_of(t * 64 + h * 32 + lo, 16), 16)
            total = part[row].astype(F32)
            for i in (128, 160, 192):
                total = total + r[pl.ds(pl.multiple_of(224 * h + i + lo, 16), 16)].astype(F32)
            x = own[m, sl].astype(F32)
            inverse = 1.0 / jnp.sqrt(jnp.mean(x * x, axis=-1, keepdims=True) + EPS)
            normed = x * inverse
            scaled = total * gain_row
            result = inverse * (scaled - normed * jnp.mean(scaled * normed, axis=-1, keepdims=True))
            res[m, sl] = (result + g[row].astype(F32)).astype(BF16)
            return carry

        lax.fori_loop(0, 2, body, 0)

    def project(g, lo, hi):
        def body(n, carry):
            r = jnp.dot(g[pl.ds(pl.multiple_of(n * 256, 256), 256)], w[...], preferred_element_type=F32).astype(BF16)
            sl = pl.ds(pl.multiple_of(n * 256, 256), 256)
            for j in range(4):
                qs[pl.ds(pl.multiple_of(j * 512 + n * 256, 256), 256)] = r[:, j * HD : (j + 1) * HD]
            kk[sl] = r[:, 512:640]
            vv[sl] = r[:, 640:768]
            return carry

        lax.fori_loop(lo, hi, body, 0)

    def back_out(g):
        def body(n, carry):
            r = lax.dot_general(
                g[pl.ds(pl.multiple_of(n * 256, 256), 256)], wout[...], nt,
                preferred_element_type=F32,
            ).astype(BF16)
            for j in range(4):
                ogs[pl.ds(pl.multiple_of(j * 512 + n * 256, 256), 256)] = r[:, j * HD : (j + 1) * HD]
            return carry

        lax.fori_loop(0, 2, body, 0)

    def mask(m):
        seg_row = segs[pl.ds(plan[p + m], 1)]
        seg_col = jnp.broadcast_to(seg_row, (128, 512)).T[:, :1]
        for b in (0, 1):
            keys = 256 * (b + 1)
            kpos = lax.broadcasted_iota(jnp.int32, (keys, 256), 0)
            qpos = lax.broadcasted_iota(jnp.int32, (keys, 256), 1) + b * 256
            allowed = (kpos <= qpos) & (seg_col[:keys] == seg_row[:, b * 256 : (b + 1) * 256])
            bias[m, 256 * b : 256 * b + keys] = jnp.where(allowed, 0.0, -1e30)

    def forward(m, lo, hi):
        def head(j, carry):
            for b in (0, 1):
                keys = 256 * (b + 1)
                sl = pl.ds(pl.multiple_of(j * 512 + b * 256, 256), 256)
                scores = lax.dot_general(kk[:keys], qs[sl], nt, preferred_element_type=F32) * scale
                scores = scores + bias[m, 256 * b : 256 * b + keys]
                weights = jnp.exp(scores - jnp.max(scores, axis=0, keepdims=True))
                weights = weights * (1.0 / jnp.sum(weights, axis=0, keepdims=True))
                probs[j, 256 * b : 256 * b + keys] = weights
            return carry

        lax.fori_loop(lo, hi, head, 0)

    def backward():
        dk_acc[...] = jnp.zeros_like(dk_acc)
        dv_acc[...] = jnp.zeros_like(dv_acc)

        def head(j, carry):
            for b in (0, 1):
                keys = 256 * (b + 1)
                sl = pl.ds(pl.multiple_of(j * 512 + b * 256, 256), 256)
                q, og = qs[sl], ogs[sl]
                weights = probs[j, 256 * b : 256 * b + keys]
                weight_grad = lax.dot_general(vv[:keys], og, nt, preferred_element_type=F32)
                delta = jnp.sum(weights * weight_grad, axis=0, keepdims=True)
                score_grad = (weights * (weight_grad - delta) * scale).astype(BF16)
                dv_acc[:keys] += jnp.dot(weights.astype(BF16), og, preferred_element_type=F32)
                dk_acc[:keys] += jnp.dot(score_grad, q, preferred_element_type=F32)
                dq = jnp.dot(kk[:keys].T, score_grad, preferred_element_type=F32)
                dqkv[j, b * 256 : (b + 1) * 256] = dq.T.astype(BF16)
            return carry

        lax.fori_loop(0, 4, head, 0)
        dqkv[4] = dk_acc[...].astype(BF16)
        dqkv[5] = dv_acc[...].astype(BF16)

    def back_in(h):
        lhs = jnp.concatenate(
            [
                jnp.concatenate([dqkv[j, 64 * i + 32 * h : 64 * i + 32 * h + 32] for j in range(6)], axis=1)
                for i in range(8)
            ],
            axis=0,
        )

        def body(n, carry):
            cols = pl.ds(pl.multiple_of(n * 512, 512), 512)
            r = lax.dot_general(lhs, w[cols], nt, preferred_element_type=F32).astype(BF16)
            for i in range(8):
                part[64 * i + 32 * h : 64 * i + 32 * h + 32, cols] = r[32 * i : 32 * i + 32]
            return carry

        lax.fori_loop(0, 8, body, 0)

    def passed(h):
        passes[h].wait_recv()
        sl = pl.ds(32 * h, 32)
        d1[rows(xh, y, h)] = jnp.where(last, lossv[sl].astype(F32), pas[sl].astype(F32)).astype(BF16)
        gd1[h].x.start()
        gd1[h].near()

    def scatter_first(sc, h):
        back_in(h)
        for c in (sc[h].b_m, sc[h].b_p, sc[h].e):
            c.start()

    last = p == 15

    for c in mirrors[0]:
        c.start()
    local[0].wait()
    gd0[0].near()
    gd0[1].near()
    mask(0)
    local[1].wait()
    for h in (0, 1):
        mirrors[0][h].wait_recv()
        gd0[h].x.start()
        norm(0, h, h0)
        gd0[h].far()
    gh0[0].near()
    gh0[1].near()
    mask(1)
    for h in (0, 1):
        gd0[h].across()
        gh0[h].x.start()
    gd0[0].last()
    for c in mirrors[1]:
        c.start()
    gh0[0].far()
    gh0[1].far()
    gh0[0].across()
    gh0[1].across()
    gd0[1].last()
    gh0[0].last()
    gh0[1].last()
    for h in (0, 1):
        mirrors[1][h].wait_recv()
        norm(1, h, h1)
        gh1[h].near()
        gh1[h].x.start()
    gd0[0].done()
    gd0[1].done()
    for c in local[2:]:
        c.wait()
    back_out(d0)
    gh0[0].done()
    gh0[1].done()
    project(h0, 0, 2)
    forward(0, 0, 4)
    gh1[0].far()
    gh1[0].across()
    backward()
    scatter_first(sc0, 0)
    gh1[1].far()
    gh1[1].across()
    scatter_first(sc0, 1)
    sc0[0].far()
    sc0[0].across()
    gh1[0].last()
    sc0[0].near()
    sc0[1].far()
    sc0[1].across()
    gh1[1].last()
    sc0[0].done()
    norm_back(0, 0, d0, r0)
    passes[0].start()
    sc0[1].near()
    passed(0)
    gh1[0].done()
    gh1[1].done()
    project(h1, 0, 1)
    sc0[1].done()
    norm_back(0, 1, d0, r0)
    passes[1].start()
    first_out = pltpu.make_async_copy(res.at[0], out.at[0, 0], lsem.at[7])
    first_out.start()
    project(h1, 1, 2)

    gd1[0].far()
    passed(1)
    gd1[0].across()
    forward(1, 0, 2)
    gd1[1].far()
    gd1[0].last()
    gd1[1].across()
    forward(1, 2, 4)
    gd1[1].last()
    for c in sc0:
        c.drain()
    for g in gd1:
        g.done()
    back_out(d1)
    backward()
    scatter_first(sc1, 0)
    scatter_first(sc1, 1)
    sc1[0].far()
    sc1[0].across()
    sc1[1].far()
    sc1[0].near()
    sc1[1].across()
    sc1[1].near()
    for h in (0, 1):
        sc1[h].done()
        norm_back(1, h, d1, r1)
    second_out = pltpu.make_async_copy(res.at[1], out.at[0, 1], lsem.at[8])
    second_out.start()
    for c in [*sc1, *gd0, *gh0, *gh1, *gd1]:
        c.drain()
    for c in [*mirrors[0], *mirrors[1], *passes]:
        c.wait_send()
    first_out.wait()
    second_out.wait()


def on_device(stashed, upstream, loss_grad, norm_gain, w_query, w_key, w_value, w_out, evicted_map, plan, segments):
    hbm = pl.BlockSpec(memory_space=pl.ANY)
    vmem = pl.BlockSpec(memory_space=pltpu.VMEM)
    smem = pl.BlockSpec(memory_space=pltpu.SMEM)
    full = pltpu.VMEM((512, 4096), BF16)
    return pl.pallas_call(
        kernel,
        name="relay_backward",
        out_shape=jax.ShapeDtypeStruct((1, 2, 64, 4096), BF16),
        in_specs=[hbm, hbm, hbm, vmem, hbm, hbm, hbm, hbm, smem, smem, vmem],
        out_specs=hbm,
        scratch_shapes=[
            pltpu.VMEM((4096, 768), BF16),
            full, full, full, full, full, full,
            pltpu.VMEM((448, 4096), BF16),
            pltpu.VMEM((448, 4096), BF16),
            pltpu.VMEM((2, 64, 4096), BF16),
            pltpu.VMEM((2, 64, 4096), BF16),
            pltpu.VMEM((64, 4096), BF16),
            pltpu.VMEM((64, 4096), BF16),
            pltpu.VMEM((2, 64, 4096), BF16),
            pltpu.VMEM((2048, HD), BF16),
            pltpu.VMEM((2048, HD), BF16),
            pltpu.VMEM((512, HD), BF16),
            pltpu.VMEM((512, HD), BF16),
            pltpu.VMEM((6, 512, HD), BF16),
            pltpu.VMEM((512, HD), F32),
            pltpu.VMEM((512, HD), F32),
            pltpu.VMEM((2, 768, 256), F32),
            pltpu.VMEM((4, 768, 256), F32),
            pltpu.SemaphoreType.DMA((9,)),
            pltpu.SemaphoreType.DMA((103,)),
            pltpu.SemaphoreType.DMA((103,)),
        ],
        compiler_params=pltpu.CompilerParams(
            collective_id=0, has_side_effects=True, vmem_limit_bytes=60 * 2**20
        ),
        cost_estimate=pl.CostEstimate(flops=20 * 10**9, bytes_accessed=16 * 2**20, transcendentals=2 * 10**6),
    )(stashed, upstream, loss_grad, norm_gain, w_query, w_key, w_value, w_out, evicted_map, plan, segments)


def solution(mesh):
    in_specs = (
        P("pipe", None, "tensor", None),
        P("pipe", "tensor", None),
        P("tensor", None),
        P("pipe", None),
        P("pipe", None, "tensor"),
        P("pipe", None, "tensor"),
        P("pipe", None, "tensor"),
        P("pipe", "tensor", None),
        P(),
        P(),
        P(),
    )
    return jax.shard_map(
        on_device, mesh=mesh, in_specs=in_specs, out_specs=P("pipe", None, "tensor", None), check_vma=False
    )
```

time: 249 us -> 204 us (0.82)
  Pallas kernels: 247 us -> 201 us
    pallas_call x1, Pallas kernels: 247 us -> 201 us  [on_device(): pl.pallas_call(kernel, name='relay_backward', out_shape=jax.ShapeDtypeStr...]
where the time goes in v1:
time: 204 us
  Pallas kernels  201 us (99%)
  local copies, waits for them, and re-layouts  2.29 us (1%)
    pallas_call x1, Pallas kernels, on_device(): pl.pallas_call(kernel, name='relay_backward', out_shape=jax.ShapeDtypeStr...  201 us

profile of v1, /device:TPU:0, one launch (start us, length us, event | category | flops | bytes accessed | tf_op | source)
XLA Modules:
  0.0 203.6 jit_solution(15601372827449891904)
XLA Ops:
  0.0 201.3 %relay_backward.1 = bf16[1,2,64,4096]{3,2,1,0:T(8,128)(2,1)} custom-call(bf16[1,2,64,4096]{3,2,1,0:T(8,128)(2,1)} %stash.1, bf16[1,64,4096]{2,1,0:T(8,128)(2,1)} %upstream.1, bf16[64,4096]{1,0:T(8,128)(2,1)} %loss.1, f32[1,4096]{1,0:T(1,128)} %gain.1, bf16[1,4096,512]{2,1,0:T(8,128)(2,1)} %wq.1, bf16[1,4096,128]{2,1,0:T(8,128)(2,1)} %wk.1, ...), custom_call_target="tpu_custom_call" | custom-call | flops 20000000000 | bytes 16777216 | tf_op jit(solution)/shard_map/relay_backward/pallas_call | solution.py:433
  201.4 2.3 %copy.13 = bf16[1,2,64,4096]{3,2,1,0:T(8,128)(2,1)} copy(bf16[1,2,64,4096]{3,2,1,0:T(8,128)(2,1)} %relay_backward.1) | data formatting | bytes 2097152
